TPU v7x, 256 devices: a whole 4x4x8 slice. The times are simulated.
256 devices in a mesh: seg: 16 (over z, core), bond: 16 (over x, y).
Axes of the slice: x: 4, y: 4, z: 8, core: 2. Of those that a mesh axis runs over, the one named last changes fastest.
Arguments:
- left_env: bfloat16 [16, 1024, 6, 1024], P('seg', 'bond'), may hold values from -0.1875 to 0.1875
- prev_left: bfloat16 [16, 1024, 1024], P('seg'), may hold values from -0.25 to 1.25
- cur_site: bfloat16 [16, 1024, 4, 1024], P('seg', 'bond'), may hold values from -6 to 6
- prev_site: bfloat16 [16, 1024, 4, 1024], P('seg', None, None, 'bond'), may hold values from -6 to 6
- hamiltonian: bfloat16 [16, 6, 6, 4, 4], P('seg'), may hold values from -1.25 to 1.25
- right_env: bfloat16 [16, 1024, 6, 1024], P('seg', 'bond'), may hold values from -0.078125 to 0.078125
- prev_right: bfloat16 [16, 1024, 1024], P('seg'), may hold values from -0.25 to 1.25
Outputs:
- new_site: bfloat16 [16, 1024, 4, 1024], P('seg', 'bond')
- center: float32 [16, 1024, 1024], P('seg', 'bond')
All inputs are finite; a program needn't handle non-finite values.
Results may differ from a plain program's by a relative error of at most 0.0054.
Values may be sent and summed in bfloat16 or wider, within the bound.
No kernel may reach another device: no remote copies, remote signals or barrier semaphores. Data moves between devices by JAX's collectives and lax.ppermute only.
A program may use at most 128 MiB of HBM per device.

v0:
```python
import math
import jax
import jax.numpy as jnp
from jax import lax
from jax.sharding import PartitionSpec as P

PHYS = 4
MPOB = 6


def shifted(block, axis, distance):
    devices = range(lax.axis_size(axis))
    route = [((i - distance) % len(devices), i) for i in devices]
    return lax.ppermute(block, axis, route)


def shards(left_env, prev_left, cur_site, prev_site, hamiltonian, right_env, prev_right):
    left_now, prev_now = shifted((left_env[0], prev_left[0]), "seg", 1)
    own_rows = left_now.shape[0]
    bond_width = left_now.shape[2]
    coupling = hamiltonian[0].astype(jnp.float32)
    current = lax.all_gather(cur_site[0], "bond", axis=0, tiled=True)
    projected = jnp.dot(
        left_now.reshape(own_rows * MPOB, bond_width),
        current.reshape(bond_width, PHYS * bond_width),
        preferred_element_type=jnp.float32,
    ).reshape(own_rows, MPOB, PHYS, bond_width)
    mixture = jnp.einsum(
        "autc,uvst->asvc", projected, coupling, precision=lax.Precision.HIGHEST
    ).astype(jnp.bfloat16)
    applied = jnp.einsum(
        "asvc,cvy->asy",
        mixture,
        lax.all_gather(right_env[0], "bond", axis=0, tiled=True),
        preferred_element_type=jnp.float32,
    )
    previous = lax.all_gather(prev_site[0], "bond", axis=2, tiled=True)
    own_left = lax.dynamic_slice_in_dim(prev_now, lax.axis_index("bond") * own_rows, own_rows, 0)
    partial_value = jnp.einsum(
        "ab,bsc->asc", own_left, previous, preferred_element_type=jnp.float32
    ).astype(jnp.bfloat16)
    second = jnp.einsum(
        "asc,cy->asy", partial_value, prev_right[0], preferred_element_type=jnp.float32
    )
    target = (2.0 * applied - second).reshape(own_rows * PHYS, bond_width)
    local_correlation = jnp.dot(
        target.T, target, precision=lax.Precision.HIGHEST, preferred_element_type=jnp.float32
    )
    correlation = lax.psum(local_correlation, "bond")
    triangle = jnp.linalg.cholesky(correlation)
    solved = jax.scipy.linalg.solve_triangular(triangle, target.T, lower=True)
    norming = math.sqrt(bond_width * PHYS)
    new_site = (solved.T * norming).astype(jnp.bfloat16).reshape(1, own_rows, PHYS, bond_width)
    offset = lax.axis_index("bond") * own_rows
    center = lax.dynamic_slice_in_dim(triangle.T, offset, own_rows, 0) / norming
    return (new_site, center[None])


def solution(mesh):
    return jax.shard_map(
        shards,
        mesh=mesh,
        in_specs=(
            P("seg", "bond", None, None),
            P("seg", None, None),
            P("seg", "bond", None, None),
            P("seg", None, None, "bond"),
            P("seg", None, None, None, None),
            P("seg", "bond", None, None),
            P("seg", None, None),
        ),
        out_specs=(P("seg", "bond", None, None), P("seg", "bond", None)),
        check_vma=False,
    )
```

profile of v0, /device:TPU:1, one launch (start us, length us, event | category | flops | bytes accessed | tf_op | source)
XLA Modules:
  0.0 756.7 jit_solution(14787921494383537855)
XLA Ops:
  8.0 2.2 copy.56
  11.0 3.0 collective-permute-start
  14.1 75.9 %all-gather.7.cloned.1.call-done = bf16[1,1024,4,1024]{3,2,0,1:T(4,128)(2,1)} async-done(((bf16[1,64,4,1024]{3,2,0,1:T(4,128)(2,1)}), bf16[1,1024,4,1024]{3,2,0,1:T(4,128)(2,1)}) %all-gather.7.cloned.1.call-update) | async-done | bytes 8388624 | tf_op jit(solution)/shard_map/all_gather | solution.py:22
  90.0 13.8 %copy.82 = bf16[1,1024,4,1024]{1,3,2,0:T(8,128)(2,1)} copy(bf16[1,1024,4,1024]{3,2,0,1:T(4,128)(2,1)} %all-gather.7.cloned.1.call-done) | data formatting | bytes 16777216 | tf_op jit(solution)/shard_map/reshape | solution.py:25
  103.9 64.7 %all-gather.11.cloned.1.call-done = bf16[1,1024,4,1024]{1,2,0,3:T(4,128)(2,1)} async-done(((bf16[1,1024,4,64]{1,2,0,3:T(4,128)(2,1)}), bf16[1,1024,4,1024]{1,2,0,3:T(4,128)(2,1)}) %all-gather.11.cloned.1.call-update) | async-done | bytes 8388624 | tf_op jit(solution)/shard_map/all_gather | solution.py:37
  168.6 13.7 %copy.57 = bf16[1,1024,4,1024]{3,1,2,0:T(8,128)(2,1)} copy(bf16[1,1024,4,1024]{1,2,0,3:T(4,128)(2,1)} %all-gather.11.cloned.1.call-done) | data formatting | bytes 16777216 | tf_op jit(solution)/shard_map/all_gather | solution.py:37
  182.3 6.3 fusion.14
  188.6 11.5 %fusion.8 = bf16[64,4,6,1024]{3,2,1,0:T(8,128)(2,1)} fusion(f32[64,6,4,1024,1]{3,0,2,1,4:T(8,128)S(1)} %fusion.14, bf16[1,6,6,4,4]{2,4,3,1,0:T(4,128)(2,1)S(1)} %copy-done.4), kind=kOutput, calls=%fused_computation.11 | convolution fusion | flops 454557696 | bytes 9438336 | tf_op jit(solution)/shard_map/autc,uvst->asvc/dot_general | solution.py:28
  200.2 65.7 %all-gather.9.cloned.1.call-done = bf16[1,1024,6,1024]{3,1,2,0:T(8,128)(2,1)} async-done(((bf16[1,64,6,1024]{3,1,2,0:T(8,128)(2,1)}), bf16[1,1024,6,1024]{3,1,2,0:T(8,128)(2,1)}) %all-gather.9.cloned.1.call-update) | async-done | bytes 12582928 | tf_op jit(solution)/shard_map/all_gather | solution.py:34
  265.9 12.8 %fusion.24 = f32[64,4,1024]{2,0,1:T(8,128)} fusion(bf16[1,1024,6,1024]{3,1,2,0:T(8,128)(2,1)} %all-gather.9.cloned.1.call-done, bf16[64,4,6,1024]{3,2,1,0:T(8,128)(2,1)} %fusion.8), kind=kOutput, calls=%fused_computation.23 | convolution fusion | flops 3221487616 | bytes 16777216 | tf_op jit(solution)/shard_map/asvc,cvy->asy/dot_general | solution.py:31
  278.7 5.8 fusion.29
  284.5 5.1 convolution_bitcast_fusion
  291.1 111.9 %all-reduce.3.cloned.1.call-done = f32[1024,1024]{0,1:T(8,128)} async-done(((f32[1024,1024]{0,1:T(8,128)}), f32[1024,1024]{0,1:T(8,128)}) %all-reduce.3.cloned.1.call-update) | async-done | bytes 4194320 | tf_op jit(solution)/shard_map/psum | solution.py:49
  403.0 5.5 copy.59
  408.5 4.4 fusion.9
  412.9 1.9 copy-done.2
  414.9 11.7 %cholesky.223 = f32[128,128]{1,0:T(8,128)S(1)} custom-call(f32[128,128]{1,0:T(8,128)S(1)} %cholesky.580), custom_call_target="Cholesky" | custom-call | tf_op jit(solution)/shard_map/jit(cholesky)/cholesky | solution.py:50
  426.6 9.8 %custom-call.63 = f32[1,128,128]{1,2,0:T(8,128)S(1)} custom-call(f32[1,128,128]{2,1,0:T(8,128)S(1)} %get-tuple-element.76), custom_call_target="InvertDiagBlocksLowerTriangular" | custom-call | tf_op jit(solution)/shard_map/jit(cholesky)/cholesky | solution.py:50
  440.2 2.5 cholesky.255
  442.7 11.9 %cholesky.244 = f32[128,128]{1,0:T(8,128)S(1)} custom-call(f32[128,128]{1,0:T(8,128)S(1)} %cholesky.584), custom_call_target="Cholesky" | custom-call | tf_op jit(solution)/shard_map/jit(cholesky)/cholesky | solution.py:50
  456.1 9.8 %custom-call.64 = f32[1,128,128]{1,2,0:T(8,128)S(1)} custom-call(f32[1,128,128]{2,1,0:T(8,128)S(1)} %get-tuple-element.73), custom_call_target="InvertDiagBlocksLowerTriangular" | custom-call | tf_op jit(solution)/shard_map/jit(cholesky)/cholesky | solution.py:50
  467.2 2.1 convolution_subtract_fusion.1
  469.3 11.7 %cholesky.468 = f32[128,128]{1,0:T(8,128)S(1)} custom-call(f32[128,128]{1,0:T(8,128)S(1)} %cholesky.589), custom_call_target="Cholesky" | custom-call | tf_op jit(solution)/shard_map/jit(cholesky)/cholesky | solution.py:50
  482.3 9.8 %custom-call.65 = f32[1,128,128]{1,2,0:T(8,128)S(1)} custom-call(f32[1,128,128]{2,1,0:T(8,128)S(1)} %get-tuple-element.70), custom_call_target="InvertDiagBlocksLowerTriangular" | custom-call | tf_op jit(solution)/shard_map/jit(cholesky)/cholesky | solution.py:50
  493.3 2.3 convolution_subtract_fusion.2
  495.6 12.1 %cholesky.487 = f32[128,128]{1,0:T(8,128)S(1)} custom-call(f32[128,128]{1,0:T(8,128)S(1)} %cholesky.594), custom_call_target="Cholesky" | custom-call | tf_op jit(solution)/shard_map/jit(cholesky)/cholesky | solution.py:50
  509.0 9.8 %custom-call.66 = f32[1,128,128]{1,2,0:T(8,128)S(1)} custom-call(f32[1,128,128]{2,1,0:T(8,128)S(1)} %get-tuple-element.67), custom_call_target="InvertDiagBlocksLowerTriangular" | custom-call | tf_op jit(solution)/shard_map/jit(cholesky)/cholesky | solution.py:50
  520.0 2.3 convolution_subtract_fusion.3
  522.3 11.7 %cholesky.506 = f32[128,128]{1,0:T(8,128)S(1)} custom-call(f32[128,128]{1,0:T(8,128)S(1)} %cholesky.599), custom_call_target="Cholesky" | custom-call | tf_op jit(solution)/shard_map/jit(cholesky)/cholesky | solution.py:50
  535.4 10.0 %custom-call.67 = f32[1,128,128]{1,2,0:T(8,128)S(1)} custom-call(f32[1,128,128]{2,1,0:T(8,128)S(1)} %get-tuple-element.64), custom_call_target="InvertDiagBlocksLowerTriangular" | custom-call | tf_op jit(solution)/shard_map/jit(cholesky)/cholesky | solution.py:50
  546.4 2.3 convolution_subtract_fusion.4
  548.7 11.7 %cholesky.526 = f32[128,128]{1,0:T(8,128)S(1)} custom-call(f32[128,128]{1,0:T(8,128)S(1)} %cholesky.604), custom_call_target="Cholesky" | custom-call | tf_op jit(solution)/shard_map/jit(cholesky)/cholesky | solution.py:50
  561.7 9.8 %custom-call.68 = f32[1,128,128]{1,2,0:T(8,128)S(1)} custom-call(f32[1,128,128]{2,1,0:T(8,128)S(1)} %get-tuple-element.61), custom_call_target="InvertDiagBlocksLowerTriangular" | custom-call | tf_op jit(solution)/shard_map/jit(cholesky)/cholesky | solution.py:50
  572.4 2.0 convolution_subtract_fusion.11
  574.5 11.9 %cholesky.546 = f32[128,128]{1,0:T(8,128)S(1)} custom-call(f32[128,128]{1,0:T(8,128)S(1)} %cholesky.609), custom_call_target="Cholesky" | custom-call | tf_op jit(solution)/shard_map/jit(cholesky)/cholesky | solution.py:50
  587.6 9.8 %custom-call.69 = f32[1,128,128]{1,2,0:T(8,128)S(1)} custom-call(f32[1,128,128]{2,1,0:T(8,128)S(1)} %get-tuple-element.58), custom_call_target="InvertDiagBlocksLowerTriangular" | custom-call | tf_op jit(solution)/shard_map/jit(cholesky)/cholesky | solution.py:50
  600.1 11.7 %cholesky.564 = f32[128,128]{1,0:T(8,128)S(1)} custom-call(f32[128,128]{1,0:T(8,128)S(1)} %convolution_subtract_fusion.13), custom_call_target="Cholesky" | custom-call | tf_op jit(solution)/shard_map/jit(cholesky)/cholesky | solution.py:50
  618.8 6.6 fusion.10
  625.3 27.4 %while.1 = (s32[]{:T(128)}, f32[1024,1024]{1,0:T(8,128)}, s32[8,2]{0,1:T(2,128)S(1)}, f32[8,128,128]{2,1,0:T(8,128)}, s32[]{:T(128)}) while((s32[]{:T(128)}, f32[1024,1024]{1,0:T(8,128)}, s32[8,2]{0,1:T(2,128)S(1)}, f32[8,128,128]{2,1,0:T(8,128)}, s32[]{:T(128)}) %tuple.65), condition=%wide.while_cond, body=%wide.while_body.sunk | while | flops 2 | bytes 132705 | solution.py:51
  625.9 2.8 bitcast_dynamic-update-slice_fusion.2
  629.4 2.8 bitcast_dynamic-update-slice_fusion.2
  632.8 2.8 bitcast_dynamic-update-slice_fusion.2
  636.2 2.8 bitcast_dynamic-update-slice_fusion.2
  639.6 2.8 bitcast_dynamic-update-slice_fusion.2
  643.1 2.8 bitcast_dynamic-update-slice_fusion.2
  646.5 2.8 bitcast_dynamic-update-slice_fusion.2
  649.9 2.8 bitcast_dynamic-update-slice_fusion.2
  652.7 79.6 %custom-call.70 = f32[8,128,128]{1,2,0:T(8,128)S(1)} custom-call(f32[8,128,128]{2,1,0:T(8,128)} %get-tuple-element.9), custom_call_target="InvertDiagBlocksLowerTriangular" | custom-call | tf_op jit(solution)/shard_map/jit(_solve_triangular)/triangular_solve | solution.py:51
  (95 shorter events, 47.1 us)
Async XLA Ops:
  7.2 271.5 %copy-start = (bf16[1,1024,1024]{2,1,0:T(8,128)(2,1)S(1)}, bf16[1,1024,1024]{2,1,0:T(8,128)(2,1)}, u32[]{:S(2)}) copy-start(bf16[1,1024,1024]{2,1,0:T(8,128)(2,1)} %param.13) | copy-start | bytes 6291460
  7.2 82.9 %all-gather.7.cloned.1.call-start = ((), (), s32[]{:S(2)}) async-start(), calls=%async_computation.1 | async-start | bytes 8912896 | tf_op jit(solution)/shard_map/all_gather | solution.py:22
  7.9 160.7 %all-gather.11.cloned.1.call-start = ((), (), s32[]{:S(2)}) async-start(), calls=%async_computation.3 | async-start | bytes 8912896 | tf_op jit(solution)/shard_map/all_gather | solution.py:37
  10.2 255.6 %all-gather.9.cloned.1.call-start = ((), (), s32[]{:S(2)}) async-start(), calls=%async_computation.2 | async-start | bytes 13369344 | tf_op jit(solution)/shard_map/all_gather | solution.py:34
  11.0 392.0 %all-reduce.3.cloned.1.call-start = ((), (), s32[]{:S(2)}) async-start(), calls=%async_computation | async-start | bytes 8388608 | tf_op jit(solution)/shard_map/psum | solution.py:49
  11.0 171.3 %collective-permute-start = (bf16[64,6,1024]{2,0,1:T(8,128)(2,1)}, bf16[64,6,1024]{2,0,1:T(8,128)(2,1)S(1)}, u32[]{:S(2)}, u32[]{:S(2)}) collective-permute-start(bf16[64,6,1024]{2,0,1:T(8,128)(2,1)} %bitcast.185), channel_id=1, source_target_pairs={{240,0},{0,16},{16,32},{32,48},{48,64},{64,80},{80,96},{96,112},{1... | collective-permute-start | bytes 2359304 | tf_op jit(solution)/shard_map/ppermute | solution.py:14
  14.1 264.6 %collective-permute-start.1 = (bf16[1024,1024]{1,0:T(8,128)(2,1)}, bf16[1024,1024]{1,0:T(8,128)(2,1)}, u32[]{:S(2)}, u32[]{:S(2)}) collective-permute-start(bf16[1024,1024]{1,0:T(8,128)(2,1)} %bitcast.184), channel_id=1, source_target_pairs={{240,0},{0,16},{16,32},{32,48},{48,64},{64,80},{80,96},{96,112},{1... | collective-permute-start | bytes 6291464 | tf_op jit(solution)/shard_map/ppermute | solution.py:14
  182.3 6.3 copy-start.4
  412.9 1.9 copy-start.2
  732.3 8.1 %copy-start.3 = (f32[8,128,128]{1,2,0:T(8,128)}, f32[8,128,128]{1,2,0:T(8,128)S(1)}, u32[]{:S(2)}) copy-start(f32[8,128,128]{1,2,0:T(8,128)S(1)} %custom-call.70) | copy-start | bytes 1572868
  740.8 9.1 %copy-start.1 = (bf16[1,1024,1024]{2,1,0:T(8,128)(2,1)S(1)}, bf16[1,1024,1024]{2,1,0:T(8,128)(2,1)}, u32[]{:S(2)}) copy-start(bf16[1,1024,1024]{2,1,0:T(8,128)(2,1)} %param.13) | copy-start | bytes 6291460
Sparse Core Ops, SparseCore 0:
  10.4 79.5 all-gather.6
  93.0 75.4 all-gather.10
  171.1 94.7 all-gather.8
  289.8 113.1 all-reduce.2
where the time goes:
time: 764 us; the launch traced here: 757 us
  waiting for transfers between devices  320 us (42%)
  other arithmetic  264 us (35%)
  matrix products  78.2 us (10%)
  local copies, waits for them, and re-layouts  71.6 us (9%)
  between operations  19.4 us (3%)
    another operation x30, other arithmetic, shards(): triangle = jnp.linalg.cholesky(correlation)  172 us
    psum x1, waiting for transfers between devices, shards(): correlation = lax.psum(local_correlation, 'bond')  112 us
    another operation x3, other arithmetic, shards(): solved = jax.scipy.linalg.solve_triangular(triangle, target.T, lower=True)  86.2 us
    all_gather x1, waiting for transfers between devices, shards(): current = lax.all_gather(cur_site[0], 'bond', axis=0, tiled=True)  75.9 us
    all_gather x1, waiting for transfers between devices, shards(): lax.all_gather(right_env[0], 'bond', axis=0, tiled=True)  65.7 us
    all_gather x1, waiting for transfers between devices, shards(): previous = lax.all_gather(prev_site[0], 'bond', axis=2, tiled=True)  64.7 us
    another operation x24, local copies, waits for them, and re-layouts  27.4 us
    another operation x14, matrix products, shards(): triangle = jnp.linalg.cholesky(correlation)  22.7 us
  transfers between devices with their start and end apart: 6, of which 4 were waited for; matrix products, arithmetic and copies ran while one was open for 8% of the time, Pallas kernels for 0%

commit v1 on v0

--- a/solution.py
+++ b/solution.py
@@ -46,7 +46,8 @@
     local_correlation = jnp.dot(
         target.T, target, precision=lax.Precision.HIGHEST, preferred_element_type=jnp.float32
     )
-    correlation = lax.psum(local_correlation, "bond")
+    pieces = lax.all_gather(local_correlation, "bond")
+    correlation = jnp.sum(pieces, axis=0)
     triangle = jnp.linalg.cholesky(correlation)
     solved = jax.scipy.linalg.solve_triangular(triangle, target.T, lower=True)
     norming = math.sqrt(bond_width * PHYS)

time: 764 us -> 1050 us (1.37)
  waiting for transfers between devices: 320 us -> 580 us
  other arithmetic: 264 us -> 287 us
    all_gather x0 -> x1, waiting for transfers between devices: none -> 372 us  [shards(): pieces = lax.all_gather(local_correlation, 'bond')]
    psum x1 -> x0, waiting for transfers between devices: 112 us -> none  [shards(): correlation = lax.psum(local_correlation, 'bond')]
    reduce_sum x0 -> x1, other arithmetic: none -> 22.9 us  [shards(): correlation = jnp.sum(pieces, axis=0)]
  transfers between devices with their start and end apart: 6 -> 6, of which waited for: 4 -> 4; matrix products, arithmetic and copies ran while one was open for 8% -> 6% of each run, Pallas kernels for 0% -> 0%
where the time goes in v1:
time: 1050 us; the launch traced here: 1040 us
  waiting for transfers between devices  580 us (55%)
  other arithmetic  287 us (27%)
  matrix products  78.2 us (7%)
  local copies, waits for them, and re-layouts  71.6 us (7%)
  between operations  19.4 us (2%)
    all_gather x1, waiting for transfers between devices, shards(): pieces = lax.all_gather(local_correlation, 'bond')  372 us
    another operation x30, other arithmetic, shards(): triangle = jnp.linalg.cholesky(correlation)  172 us
    another operation x3, other arithmetic, shards(): solved = jax.scipy.linalg.solve_triangular(triangle, target.T, lower=True)  86.2 us
    all_gather x1, waiting for transfers between devices, shards(): current = lax.all_gather(cur_site[0], 'bond', axis=0, tiled=True)  75.9 us
    all_gather x1, waiting for transfers between devices, shards(): lax.all_gather(right_env[0], 'bond', axis=0, tiled=True)  65.7 us
    all_gather x1, waiting for transfers between devices, shards(): previous = lax.all_gather(prev_site[0], 'bond', axis=2, tiled=True)  64.7 us
    another operation x24, local copies, waits for them, and re-layouts  27.3 us
    reduce_sum x1, other arithmetic, shards(): correlation = jnp.sum(pieces, axis=0)  22.9 us
  transfers between devices with their start and end apart: 6, of which 4 were waited for; matrix products, arithmetic and copies ran while one was open for 6% of the time, Pallas kernels for 0%

profile of v1, /device:TPU:1, one launch (start us, length us, event | category | flops | bytes accessed | tf_op | source)
XLA Modules:
  0.0 1039.7 jit_solution(12966754765764836906)
XLA Ops:
  8.0 2.2 copy.53
  11.0 3.0 collective-permute-start
  14.1 75.9 %all-gather.9.cloned.1.call-done = bf16[1,1024,4,1024]{3,2,0,1:T(4,128)(2,1)} async-done(((bf16[1,64,4,1024]{3,2,0,1:T(4,128)(2,1)}), bf16[1,1024,4,1024]{3,2,0,1:T(4,128)(2,1)}) %all-gather.9.cloned.1.call-update) | async-done | bytes 8388624 | tf_op jit(solution)/shard_map/all_gather | solution.py:22
  90.0 13.8 %copy.77 = bf16[1,1024,4,1024]{1,3,2,0:T(8,128)(2,1)} copy(bf16[1,1024,4,1024]{3,2,0,1:T(4,128)(2,1)} %all-gather.9.cloned.1.call-done) | data formatting | bytes 16777216 | tf_op jit(solution)/shard_map/reshape | solution.py:25
  103.9 64.7 %all-gather.13.cloned.1.call-done = bf16[1,1024,4,1024]{1,2,0,3:T(4,128)(2,1)} async-done(((bf16[1,1024,4,64]{1,2,0,3:T(4,128)(2,1)}), bf16[1,1024,4,1024]{1,2,0,3:T(4,128)(2,1)}) %all-gather.13.cloned.1.call-update) | async-done | bytes 8388624 | tf_op jit(solution)/shard_map/all_gather | solution.py:37
  168.6 13.7 %copy.54 = bf16[1,1024,4,1024]{3,1,2,0:T(8,128)(2,1)} copy(bf16[1,1024,4,1024]{1,2,0,3:T(4,128)(2,1)} %all-gather.13.cloned.1.call-done) | data formatting | bytes 16777216 | tf_op jit(solution)/shard_map/all_gather | solution.py:37
  182.3 6.3 fusion.14
  188.6 11.5 %fusion.8 = bf16[64,4,6,1024]{3,2,1,0:T(8,128)(2,1)} fusion(f32[64,6,4,1024,1]{3,0,2,1,4:T(8,128)S(1)} %fusion.14, bf16[1,6,6,4,4]{2,4,3,1,0:T(4,128)(2,1)S(1)} %copy-done.4), kind=kOutput, calls=%fused_computation.11 | convolution fusion | flops 454557696 | bytes 9438336 | tf_op jit(solution)/shard_map/autc,uvst->asvc/dot_general | solution.py:28
  200.2 65.7 %all-gather.11.cloned.1.call-done = bf16[1,1024,6,1024]{3,1,2,0:T(8,128)(2,1)} async-done(((bf16[1,64,6,1024]{3,1,2,0:T(8,128)(2,1)}), bf16[1,1024,6,1024]{3,1,2,0:T(8,128)(2,1)}) %all-gather.11.cloned.1.call-update) | async-done | bytes 12582928 | tf_op jit(solution)/shard_map/all_gather | solution.py:34
  265.9 12.8 %fusion.24 = f32[64,4,1024]{2,0,1:T(8,128)} fusion(bf16[1,1024,6,1024]{3,1,2,0:T(8,128)(2,1)} %all-gather.11.cloned.1.call-done, bf16[64,4,6,1024]{3,2,1,0:T(8,128)(2,1)} %fusion.8), kind=kOutput, calls=%fused_computation.23 | convolution fusion | flops 3221487616 | bytes 16777216 | tf_op jit(solution)/shard_map/asvc,cvy->asy/dot_general | solution.py:31
  278.7 5.8 fusion.29
  284.5 5.1 convolution_bitcast_fusion
  291.0 372.1 %all-gather.15.cloned.1.call-done = f32[16384,1024]{1,0:T(8,128)} async-done(((f32[1024,1024]{1,0:T(8,128)}), f32[16384,1024]{1,0:T(8,128)}) %all-gather.15.cloned.1.call-update) | async-done | bytes 67108880 | tf_op jit(solution)/shard_map/all_gather | solution.py:49
  663.1 22.9 %reduce_sum.9 = f32[1024,1024]{1,0:T(8,128)} reduce(f32[16,1024,1024]{2,1,0:T(8,128)} %bitcast.24, f32[]{:T(128)} %constant.282.clone.1), dimensions={0}, to_apply=%region_0.0 | reduce | flops 15728640 | bytes 71303168 | tf_op jit(solution)/shard_map/reduce_sum | solution.py:50
  686.1 5.5 copy.55
  691.6 4.4 fusion.9
  698.0 11.7 %cholesky.223 = f32[128,128]{1,0:T(8,128)S(1)} custom-call(f32[128,128]{1,0:T(8,128)S(1)} %cholesky.580), custom_call_target="Cholesky" | custom-call | tf_op jit(solution)/shard_map/jit(cholesky)/cholesky | solution.py:51
  709.7 2.5 cholesky.255
  712.2 9.8 custom-call.63
  725.8 11.9 %cholesky.244 = f32[128,128]{1,0:T(8,128)S(1)} custom-call(f32[128,128]{1,0:T(8,128)S(1)} %cholesky.584), custom_call_target="Cholesky" | custom-call | tf_op jit(solution)/shard_map/jit(cholesky)/cholesky | solution.py:51
  739.2 9.8 custom-call.64
  750.3 2.1 convolution_subtract_fusion.1
  752.4 11.7 %cholesky.468 = f32[128,128]{1,0:T(8,128)S(1)} custom-call(f32[128,128]{1,0:T(8,128)S(1)} %cholesky.589), custom_call_target="Cholesky" | custom-call | tf_op jit(solution)/shard_map/jit(cholesky)/cholesky | solution.py:51
  765.4 9.8 custom-call.65
  776.4 2.3 convolution_subtract_fusion.2
  778.7 12.1 %cholesky.487 = f32[128,128]{1,0:T(8,128)S(1)} custom-call(f32[128,128]{1,0:T(8,128)S(1)} %cholesky.594), custom_call_target="Cholesky" | custom-call | tf_op jit(solution)/shard_map/jit(cholesky)/cholesky | solution.py:51
  792.1 9.8 custom-call.66
  803.0 2.3 convolution_subtract_fusion.3
  805.4 11.7 %cholesky.506 = f32[128,128]{1,0:T(8,128)S(1)} custom-call(f32[128,128]{1,0:T(8,128)S(1)} %cholesky.599), custom_call_target="Cholesky" | custom-call | tf_op jit(solution)/shard_map/jit(cholesky)/cholesky | solution.py:51
  818.5 10.0 custom-call.67
  829.5 2.3 convolution_subtract_fusion.4
  831.8 11.7 %cholesky.526 = f32[128,128]{1,0:T(8,128)S(1)} custom-call(f32[128,128]{1,0:T(8,128)S(1)} %cholesky.604), custom_call_target="Cholesky" | custom-call | tf_op jit(solution)/shard_map/jit(cholesky)/cholesky | solution.py:51
  844.8 9.8 custom-call.68
  855.5 2.0 convolution_subtract_fusion.11
  857.6 11.9 %cholesky.546 = f32[128,128]{1,0:T(8,128)S(1)} custom-call(f32[128,128]{1,0:T(8,128)S(1)} %cholesky.609), custom_call_target="Cholesky" | custom-call | tf_op jit(solution)/shard_map/jit(cholesky)/cholesky | solution.py:51
  870.7 9.8 custom-call.69
  883.2 11.7 %cholesky.564 = f32[128,128]{1,0:T(8,128)S(1)} custom-call(f32[128,128]{1,0:T(8,128)S(1)} %convolution_subtract_fusion.13), custom_call_target="Cholesky" | custom-call | tf_op jit(solution)/shard_map/jit(cholesky)/cholesky | solution.py:51
  901.8 6.6 fusion.10
  908.4 27.4 %while.1 = (s32[]{:T(128)}, f32[1024,1024]{1,0:T(8,128)}, s32[8,2]{0,1:T(2,128)S(1)}, f32[8,128,128]{2,1,0:T(8,128)}, s32[]{:T(128)}) while((s32[]{:T(128)}, f32[1024,1024]{1,0:T(8,128)}, s32[8,2]{0,1:T(2,128)S(1)}, f32[8,128,128]{2,1,0:T(8,128)}, s32[]{:T(128)}) %tuple.65), condition=%wide.while_cond, body=%wide.while_body.sunk | while | flops 2 | bytes 132705 | solution.py:52
  909.0 2.8 bitcast_dynamic-update-slice_fusion.2
  912.5 2.8 bitcast_dynamic-update-slice_fusion.2
  915.9 2.8 bitcast_dynamic-update-slice_fusion.2
  919.3 2.8 bitcast_dynamic-update-slice_fusion.2
  922.7 2.8 bitcast_dynamic-update-slice_fusion.2
  926.2 2.8 bitcast_dynamic-update-slice_fusion.2
  929.6 2.8 bitcast_dynamic-update-slice_fusion.2
  933.0 2.8 bitcast_dynamic-update-slice_fusion.2
  935.8 79.6 %custom-call.70 = f32[8,128,128]{1,2,0:T(8,128)S(1)} custom-call(f32[8,128,128]{2,1,0:T(8,128)} %get-tuple-element.9), custom_call_target="InvertDiagBlocksLowerTriangular" | custom-call | tf_op jit(solution)/shard_map/jit(_solve_triangular)/triangular_solve | solution.py:52
  (96 shorter events, 49.0 us)
Async XLA Ops:
  7.2 271.5 %copy-start = (bf16[1,1024,1024]{2,1,0:T(8,128)(2,1)S(1)}, bf16[1,1024,1024]{2,1,0:T(8,128)(2,1)}, u32[]{:S(2)}) copy-start(bf16[1,1024,1024]{2,1,0:T(8,128)(2,1)} %param.13) | copy-start | bytes 6291460
  7.2 82.9 %all-gather.9.cloned.1.call-start = ((), (), s32[]{:S(2)}) async-start(), calls=%async_computation | async-start | bytes 8912896 | tf_op jit(solution)/shard_map/all_gather | solution.py:22
  7.9 160.7 %all-gather.13.cloned.1.call-start = ((), (), s32[]{:S(2)}) async-start(), calls=%async_computation.2 | async-start | bytes 8912896 | tf_op jit(solution)/shard_map/all_gather | solution.py:37
  10.2 255.6 %all-gather.11.cloned.1.call-start = ((), (), s32[]{:S(2)}) async-start(), calls=%async_computation.1 | async-start | bytes 13369344 | tf_op jit(solution)/shard_map/all_gather | solution.py:34
  11.0 652.2 %all-gather.15.cloned.1.call-start = ((), (), s32[]{:S(2)}) async-start(), calls=%async_computation.3 | async-start | bytes 71303168 | tf_op jit(solution)/shard_map/all_gather | solution.py:49
  11.0 171.3 %collective-permute-start = (bf16[64,6,1024]{2,0,1:T(8,128)(2,1)}, bf16[64,6,1024]{2,0,1:T(8,128)(2,1)S(1)}, u32[]{:S(2)}, u32[]{:S(2)}) collective-permute-start(bf16[64,6,1024]{2,0,1:T(8,128)(2,1)} %bitcast.186), channel_id=1, source_target_pairs={{240,0},{0,16},{16,32},{32,48},{48,64},{64,80},{80,96},{96,112},{1... | collective-permute-start | bytes 2359304 | tf_op jit(solution)/shard_map/ppermute | solution.py:14
  14.1 264.6 %collective-permute-start.1 = (bf16[1024,1024]{1,0:T(8,128)(2,1)}, bf16[1024,1024]{1,0:T(8,128)(2,1)}, u32[]{:S(2)}, u32[]{:S(2)}) collective-permute-start(bf16[1024,1024]{1,0:T(8,128)(2,1)} %bitcast.185), channel_id=1, source_target_pairs={{240,0},{0,16},{16,32},{32,48},{48,64},{64,80},{80,96},{96,112},{1... | collective-permute-start | bytes 6291464 | tf_op jit(solution)/shard_map/ppermute | solution.py:14
  182.3 6.3 copy-start.4
  696.0 1.9 copy-start.2
  1015.4 8.1 copy-start.3
  1023.9 9.1 copy-start.1
Sparse Core Ops, SparseCore 0:
  10.4 79.5 all-gather.8
  93.0 75.4 all-gather.12
  171.1 94.7 all-gather.10
  289.7 373.3 all-gather.14
